TPU v7x, 32 devices: a whole 2x2x4 slice. The times are simulated.
32 devices in a mesh: blk: 8 (over y, x, core), sub: 4 (over z).
Axes of the slice: x: 2, y: 2, z: 4, core: 2. Of those that a mesh axis runs over, the one named last changes fastest.
Arguments:
- tracer: float32 [80, 2, 64, 1024], P(None, None, 'sub', 'blk'), may hold values from -6 to 6
- velocity: float32 [2, 80, 64, 1024], P(None, None, 'sub', 'blk'), may hold values from -0.3 to 0.3
- kappa: float32 [79, 64, 1024], P(None, 'sub', 'blk'), may hold values from 0.02 to 200
- kmt: int32 [64, 1024], P('sub', 'blk'), may hold values from 1 to 80
- land_mask: int32 [64, 1024], P('sub', 'blk'), may hold values 0 or 1
- atm_flux: float32 [2, 196608], P(None, ('blk', 'sub')), may hold values from -6 to 6
- remap_weight: bfloat16 [2048, 128, 128], P(('blk', 'sub')), may hold values from -0.5 to 0.5
- remap_dest: int32 [2048, 1], P(('blk', 'sub')), may hold values from 0 to 31; in each aligned block of 64 rows (0 to 63, 64 to 127, ...) at most 4 rows name the same one
- remap_src_block: int32 [2048], P(('blk', 'sub')), may hold values from 0 to 47
- remap_dst_block: int32 [2048], P(('blk', 'sub')), may hold values from 0 to 15
Outputs:
- tracer_out: float32 [80, 2, 64, 1024], P(None, None, 'sub', 'blk')
- atmosphere_surface_tracer: float32 [2, 196608], P(None, ('blk', 'sub'))
Inputs may be any that keep to these rules, and one draw needn't show every extreme that they name: `remap_dest`: among the 64 tiles of one device, no destination device is named more than 4 times, a bound that some block reaches.
All inputs are finite; a program needn't handle non-finite values. No bound on the sum of `land_mask` on one device may be relied on, other than what follows from the above.
Results may differ from a plain program's by a relative error of at most 0.0003.
Values sent between devices are 32-bit elements; how exact they have to be, the bound alone decides.
A program may use at most 192 MiB of HBM per device.

v0:
```python
import functools

import jax
import jax.numpy as jnp
from jax import lax
from jax.experimental import pallas as pl
from jax.experimental.pallas import tpu as pltpu
from jax.sharding import PartitionSpec as P

NSTEP = 4
FORCE = 0.25
HIGH = lax.Precision.HIGHEST
MESH = pl.DeviceIdType.MESH
UNROLL = 8


def ocean_kernel(
    n_blk, n_sub, tracer, velocity, kappa, kmt, land, flux, out,
    cc, cw, ce, cn, cs, md, gg, inv, col_out, row_out, col_in, row_in,
    col_send, row_send, col_recv, row_recv,
):
    levels, ntr, rows, cols = tracer.shape
    blk, sub = lax.axis_index("blk"), lax.axis_index("sub")
    east, west = lax.rem(blk + 1, n_blk), lax.rem(blk + n_blk - 1, n_blk)
    has_north, has_south = sub < n_sub - 1, sub > 0
    north, south = lax.rem(sub + 1, n_sub), lax.rem(sub + n_sub - 1, n_sub)
    lane = lax.broadcasted_iota(jnp.int32, (rows, cols), 1)
    row = lax.broadcasted_iota(jnp.int32, (rows, cols), 0)
    unroll = UNROLL if levels % UNROLL == 0 else 1
    zero = jnp.zeros((rows, cols), jnp.float32)

    barrier = pltpu.get_barrier_semaphore()
    pl.semaphore_signal(barrier, inc=1, device_id=(east, sub), device_id_type=MESH)
    pl.semaphore_signal(barrier, inc=1, device_id=(west, sub), device_id_type=MESH)

    @pl.when(has_north)
    def _():
        pl.semaphore_signal(barrier, inc=1, device_id=(blk, north), device_id_type=MESH)

    @pl.when(has_south)
    def _():
        pl.semaphore_signal(barrier, inc=1, device_id=(blk, south), device_id_type=MESH)

    pl.semaphore_wait(barrier, 2 + has_north.astype(jnp.int32) + has_south.astype(jnp.int32))

    def col_copy(step, side, count):
        return pltpu.make_async_remote_copy(
            src_ref=col_out.at[step, side, pl.ds(0, count)],
            dst_ref=col_in.at[step, side, pl.ds(0, count)],
            send_sem=col_send.at[step, side],
            recv_sem=col_recv.at[step, side],
            device_id=(east if side else west, sub),
            device_id_type=MESH,
        )

    def row_copy(step, side, count):
        return pltpu.make_async_remote_copy(
            src_ref=row_out.at[step, side, pl.ds(0, count)],
            dst_ref=row_in.at[step, side, pl.ds(0, count)],
            send_sem=row_send.at[step, side],
            recv_sem=row_recv.at[step, side],
            device_id=(blk, north if side else south),
            device_id_type=MESH,
        )

    def send(step, count):
        @pl.when(has_south)
        def _():
            row_copy(step, 0, count).start()

        @pl.when(has_north)
        def _():
            row_copy(step, 1, count).start()

        col_copy(step, 0, count).start()
        col_copy(step, 1, count).start()

    def receive(step, count):
        col_copy(step, 0, count).wait_recv()
        col_copy(step, 1, count).wait_recv()

        @pl.when(has_north)
        def _():
            row_copy(step, 0, count).wait_recv()

        @pl.when(has_south)
        def _():
            row_copy(step, 1, count).wait_recv()

    def finish(step, count):
        col_copy(step, 0, count).wait_send()
        col_copy(step, 1, count).wait_send()

        @pl.when(has_south)
        def _():
            row_copy(step, 0, count).wait_send()

        @pl.when(has_north)
        def _():
            row_copy(step, 1, count).wait_send()

    def loop(body, init, down=False):
        def group(i, carry):
            for j in range(unroll):
                k = i * unroll + j
                carry = body(levels - 1 - k if down else k, carry)
            return carry

        return lax.fori_loop(0, levels // unroll, group, init)

    def put_col(packed, value, k, side):
        shift = k if side == 0 else lax.rem(k + 1, cols)
        return jnp.where(lane == k, pltpu.roll(value, shift, 1), packed)

    def west_of(value, halo, k):
        return jnp.where(lane == 0, pltpu.roll(halo, lax.rem(cols - k, cols), 1), pltpu.roll(value, 1, 1))

    def east_of(value, halo, k):
        return jnp.where(lane == cols - 1, pltpu.roll(halo, cols - 1 - k, 1), pltpu.roll(value, cols - 1, 1))

    def north_of(value, halo):
        return jnp.where(row == rows - 1, halo, pltpu.roll(value, rows - 1, 0))

    def south_of(value, halo):
        return jnp.where(row == 0, halo, pltpu.roll(value, 1, 0))

    def pack_first(k, carry):
        carry = list(carry)
        for f in range(ntr + 1):
            value = tracer[k, f] if f < ntr else velocity[0, k]
            across = value if f < ntr else velocity[1, k]
            for side in range(2):
                carry[2 * f + side] = put_col(carry[2 * f + side], value, k, side)
            row_out[0, 0, f, pl.ds(k, 1), :] = across[:1]
            row_out[0, 1, f, pl.ds(k, 1), :] = across[rows - 1:]
        return tuple(carry)

    packed = loop(pack_first, (zero,) * (2 * ntr + 2))
    for f in range(ntr + 1):
        for side in range(2):
            col_out[0, side, f] = packed[2 * f + side]
    send(0, ntr + 1)

    @pl.when(jnp.logical_not(has_north))
    def _():
        row_in[:, 0] = jnp.zeros(row_in.shape[:1] + row_in.shape[2:], jnp.float32)

    @pl.when(jnp.logical_not(has_south))
    def _():
        row_in[:, 1] = jnp.zeros(row_in.shape[:1] + row_in.shape[2:], jnp.float32)

    wet_depth = jnp.where(land[...] > 0, kmt[...], 0)

    def factor(k, carry):
        below, hold = carry
        above = jnp.where(k < wet_depth, kappa[jnp.maximum(k - 1, 0)], 0.0)
        above = jnp.where(k > 0, above, 0.0)
        part = 1.0 + below * hold
        scale = 1.0 / (above + part)
        inv[k] = scale
        gg[k] = above * scale
        md[k] = below * scale
        return above, part * scale

    loop(factor, (zero, zero), down=True)
    receive(0, ntr + 1)

    wall_north = jnp.where((row == rows - 1) & jnp.logical_not(has_north), 0.0, 0.5)
    wall_south = jnp.where((row == 0) & jnp.logical_not(has_south), 0.0, 0.5)
    u_east, u_west = col_in[0, 0, ntr], col_in[0, 1, ntr]

    def stencil(k, carry):
        u, v = velocity[0, k], velocity[1, k]
        v_north = row_in[0, 0, ntr, pl.ds(k, 1), :]
        v_south = row_in[0, 1, ntr, pl.ds(k, 1), :]
        e = 0.5 * (u + east_of(u, u_east, k))
        w = 0.5 * (west_of(u, u_west, k) + u)
        n = wall_north * (v + north_of(v, v_north))
        s = wall_south * (south_of(v, v_south) + v)
        scale = inv[k]
        wet = jnp.where(k < wet_depth, scale, 0.0)
        cc[k] = scale + wet * (
            (jnp.minimum(w, 0.0) - jnp.maximum(e, 0.0)) + (jnp.minimum(s, 0.0) - jnp.maximum(n, 0.0))
        )
        cw[k] = wet * jnp.maximum(w, 0.0)
        ce[k] = -wet * jnp.minimum(e, 0.0)
        cs[k] = wet * jnp.maximum(s, 0.0)
        cn[k] = -wet * jnp.minimum(n, 0.0)
        return carry

    loop(stencil, 0)
    surface = jnp.where(land[...] > 0, FORCE, 0.0) * inv[0]

    for step in range(NSTEP):
        if step:
            receive(step, ntr)
        state = tracer if step == 0 else out
        halo_e = [col_in[step, 0, f] for f in range(ntr)]
        halo_w = [col_in[step, 1, f] for f in range(ntr)]

        def forward(k, carry):
            now = []
            for f in range(ntr):
                value = state[k, f]
                acc = cc[k] * value + md[k] * carry[f]
                acc += cw[k] * west_of(value, halo_w[f], k)
                acc += ce[k] * east_of(value, halo_e[f], k)
                acc += cn[k] * north_of(value, row_in[step, 0, f, pl.ds(k, 1), :])
                acc += cs[k] * south_of(value, row_in[step, 1, f, pl.ds(k, 1), :])
                out[k, f] = acc
                now.append(acc)
            return tuple(now)

        top = loop(forward, (zero,) * ntr, down=True)
        for f in range(ntr):
            out[0, f] = top[f] + surface * flux[f]

        last = step == NSTEP - 1

        def backward(k, carry):
            carry = list(carry)
            for f in range(ntr):
                value = out[k, f] + gg[k] * carry[f]
                out[k, f] = value
                carry[f] = value
                if not last:
                    for side in range(2):
                        at = ntr + 2 * f + side
                        carry[at] = put_col(carry[at], value, k, side)
                    row_out[step + 1, 0, f, pl.ds(k, 1), :] = value[:1]
                    row_out[step + 1, 1, f, pl.ds(k, 1), :] = value[rows - 1:]
            return tuple(carry)

        done = loop(backward, (zero,) * (ntr if last else 3 * ntr))
        if not last:
            for f in range(ntr):
                for side in range(2):
                    col_out[step + 1, side, f] = done[ntr + 2 * f + side]
            send(step + 1, ntr)

    for step in range(NSTEP):
        finish(step, ntr + 1 if step == 0 else ntr)


def ocean(n_blk, n_sub, tracer, velocity, kappa, kmt, land, flux):
    levels, ntr, rows, cols = tracer.shape
    field = pltpu.VMEM((levels, rows, cols), jnp.float32)
    vmem = pl.BlockSpec(memory_space=pltpu.VMEM)
    return pl.pallas_call(
        functools.partial(ocean_kernel, n_blk, n_sub),
        out_shape=jax.ShapeDtypeStruct(tracer.shape, jnp.float32),
        in_specs=[vmem] * 6,
        out_specs=vmem,
        scratch_shapes=[field] * 8
        + [
            pltpu.VMEM((NSTEP, 2, ntr + 1, rows, cols), jnp.float32),
            pltpu.VMEM((NSTEP, 2, ntr + 1, levels, cols), jnp.float32),
            pltpu.VMEM((NSTEP, 2, ntr + 1, rows, cols), jnp.float32),
            pltpu.VMEM((NSTEP, 2, ntr + 1, levels, cols), jnp.float32),
            pltpu.SemaphoreType.DMA((NSTEP, 2)),
            pltpu.SemaphoreType.DMA((NSTEP, 2)),
            pltpu.SemaphoreType.DMA((NSTEP, 2)),
            pltpu.SemaphoreType.DMA((NSTEP, 2)),
        ],
        compiler_params=pltpu.CompilerParams(
            collective_id=0, has_side_effects=True, vmem_limit_bytes=40 * 1024 * 1024
        ),
        name="ocean",
    )(tracer, velocity, kappa, kmt, land, flux)


def local(
    tracer, velocity, kappa, kmt, land_mask, atm_flux, remap_weight, remap_dest, remap_src_block, remap_dst_block
):
    levels, ntracer, rows, cols = tracer.shape
    n_blk = lax.axis_size("blk")
    n_sub = lax.axis_size("sub")
    devices = n_blk * n_sub
    tiles = remap_weight.shape[0]
    capacity = max(2, 2 * tiles // devices)
    slots = devices * capacity
    atm_blocks = atm_flux.shape[1] // cols
    weights32 = remap_weight.astype(jnp.float32)
    src_pick = (remap_src_block[:, None] == jnp.arange(atm_blocks, dtype=jnp.int32)[None]).astype(jnp.float32)
    atm_local = atm_flux.reshape(ntracer, atm_blocks, cols)
    blocks = jnp.einsum("tk,fkc->tfc", src_pick, atm_local, precision=HIGH)
    contrib = jnp.einsum("tfa,tab->tfb", blocks, weights32, precision=HIGH)
    dest = remap_dest[:, 0]
    same = (dest[:, None] == dest[None, :]) & (
        jnp.arange(tiles, dtype=jnp.int32)[:, None] > jnp.arange(tiles, dtype=jnp.int32)[None]
    )
    rank = jnp.sum(same.astype(jnp.int32), axis=1)
    slot_of = dest * capacity + rank
    place = (slot_of[:, None] == jnp.arange(slots, dtype=jnp.int32)[None]).astype(jnp.float32)
    named = jnp.broadcast_to(remap_dst_block.astype(jnp.float32)[:, None, None], (tiles, 1, cols))
    outgoing = jnp.einsum("ts,tfc->sfc", place, jnp.concatenate([contrib, named], axis=1), precision=HIGH)
    incoming = lax.all_to_all(
        outgoing.reshape(devices, capacity, ntracer + 1, cols),
        ("blk", "sub"),
        split_axis=0,
        concat_axis=0,
        tiled=True,
    ).reshape(slots, ntracer + 1, cols)
    got_rows = incoming[:, ntracer, 0].astype(jnp.int32)
    row_pick = (got_rows[:, None] == jnp.arange(rows, dtype=jnp.int32)[None]).astype(jnp.float32)
    ocean_flux = jnp.einsum("sr,sfc->frc", row_pick, incoming[:, :ntracer], precision=HIGH)
    ocean_state = ocean(n_blk, n_sub, tracer, velocity, kappa, kmt, land_mask, ocean_flux)
    surface_rows = jnp.einsum("sr,frc->sfc", row_pick, ocean_state[0], precision=HIGH)
    returned = lax.all_to_all(
        surface_rows.reshape(devices, capacity, ntracer, cols),
        ("blk", "sub"),
        split_axis=0,
        concat_axis=0,
        tiled=True,
    )
    returned = returned.reshape(slots, ntracer, cols)
    tile_values = jnp.einsum("ts,sfc->tfc", place, returned, precision=HIGH)
    back = jnp.einsum("tfb,tab->tfa", tile_values, weights32, precision=HIGH)
    atmosphere_return = jnp.einsum("tk,tfa->fka", src_pick, back, precision=HIGH)
    return (ocean_state, atmosphere_return.reshape(ntracer, atm_blocks * cols))


def solution(mesh):
    return jax.shard_map(
        local,
        mesh=mesh,
        in_specs=(
            P(None, None, "sub", "blk"),
            P(None, None, "sub", "blk"),
            P(None, "sub", "blk"),
            P("sub", "blk"),
            P("sub", "blk"),
            P(None, ("blk", "sub")),
            P(("blk", "sub"), None, None),
            P(("blk", "sub"), None),
            P(("blk", "sub")),
            P(("blk", "sub")),
        ),
        out_specs=(P(None, None, "sub", "blk"), P(None, ("blk", "sub"))),
        check_vma=False,
    )
```

profile of v0, /device:TPU:0, one launch (start us, length us, event | category | flops | bytes accessed | tf_op | source)
XLA Modules:
  0.0 88.7 jit_solution(15178441093108974454)
XLA Ops:
  0.6 0.0 copy-start
  0.6 1.0 %convert_reduce_fusion = s32[64]{0:T(128)S(1)} fusion(s32[64]{0:T(128)} %bitcast.53), kind=kLoop, calls=%fused_computation.18 | loop fusion | flops 20416 | bytes 512 | tf_op jit(solution)/shard_map/reduce_sum | solution.py:292
  1.6 0.7 fusion.32
  2.3 0.7 convert_element_type.25
  3.0 1.0 %fusion.8 = f32[64,2,128]{2,0,1:T(8,128)S(1)} fusion(f32[1,2,48,128]{3,1,2,0:T(2,128)} %bitcast.51, s32[64]{0:T(128)} %param.18), kind=kOutput, calls=%fused_computation.13 | convolution fusion | flops 9440256 | bytes 114944 | tf_op jit(solution)/shard_map/tk,fkc->tfc/dot_general | solution.py:286
  4.0 0.0 copy-done
  4.0 0.0 copy-start.1
  4.0 0.0 copy-start.4
  4.1 0.0 copy-start.5
  4.1 1.7 %fusion.6 = f32[64,2,128]{2,1,0:T(2,128)S(1)} fusion(bf16[64,128,128]{2,1,0:T(8,128)(2,1)S(1)} %copy-done, f32[64,2,128]{2,0,1:T(8,128)S(1)} %fusion.8), kind=kOutput, calls=%fused_computation.10 | convolution fusion | flops 25165824 | bytes 2228224 | tf_op jit(solution)/shard_map/tfa,tab->tfb/dot_general | solution.py:287
  5.8 0.1 broadcast_in_dim.2
  5.9 0.1 pad_maximum_fusion
  6.0 0.4 fusion
  6.4 16.4 %all_to_all.10 = f32[32,4,3,128]{3,1,2,0:T(4,128)S(1)} all-to-all(f32[32,4,3,128]{3,1,2,0:T(4,128)S(1)} %copy.26), channel_id=1, replica_groups=mesh['blk'=8,'sub'=4] {'blk','sub'}, dimensions={0} | all-to-all | bytes 393216 | tf_op jit(solution)/shard_map/all_to_all | solution.py:297
  22.9 0.1 fusion.2
  23.0 0.2 convolution_bitcast_fusion.1.flux
  23.2 0.1 convert_element_type.28
  23.3 0.1 copy.28
  23.3 0.0 copy-done.1
  23.3 0.0 copy-done.4
  23.4 0.0 copy-done.5
  23.4 0.0 copy-start.2
  23.4 1.3 %copy-done.2 = f32[2,80,16,128]{3,2,1,0:T(8,128)S(1)} copy-done((f32[2,80,16,128]{3,2,1,0:T(8,128)S(1)}, f32[2,80,16,128]{3,2,1,0:T(8,128)}, u32[]{:S(2)}) %copy-start.2) | copy-done | bytes 1310744
  24.7 0.0 copy-start.3
  24.7 1.1 %copy-done.3 = f32[79,16,128]{2,1,0:T(8,128)S(1)} copy-done((f32[79,16,128]{2,1,0:T(8,128)S(1)}, f32[79,16,128]{2,1,0:T(8,128)}, u32[]{:S(2)}) %copy-start.3) | copy-done | bytes 647192
  25.8 45.9 %ocean.1 = f32[80,2,16,128]{3,2,1,0:T(8,128)S(1)} custom-call(f32[80,2,16,128]{3,2,1,0:T(8,128)S(1)} %copy-done.1, f32[2,80,16,128]{3,2,1,0:T(8,128)S(1)} %copy-done.2, f32[79,16,128]{2,1,0:T(8,128)S(1)} %copy-done.3, s32[16,128]{1,0:T(8,128)S(1)} %copy-done.4, s32[16,128]{1,0:T(8,128)S(1)} %copy-done.5, f32[2,16,128]{2,1,0:T(8,128)S(1)} %convolution_bitcast_fusion.1.flux), custom_call_target="tpu_custom_call" | custom-call | tf_op jit(solution)/shard_map/ocean/pallas_call | solution.py:249
  71.6 0.0 copy-start.6
  71.6 0.3 fusion.17
  71.9 0.1 copy.29
  72.0 11.2 %all_to_all.11 = f32[32,4,2,128]{3,2,1,0:T(2,128)S(1)} all-to-all(f32[32,4,2,128]{3,2,1,0:T(2,128)S(1)} %copy.29), channel_id=1, replica_groups=mesh['blk'=8,'sub'=4] {'blk','sub'}, dimensions={0} | all-to-all | bytes 262144 | tf_op jit(solution)/shard_map/all_to_all | solution.py:309
  83.2 0.2 fusion.13
  83.5 3.3 %fusion.4 = f32[64,2,128]{2,1,0:T(2,128)S(1)} fusion(bf16[64,128,128]{2,1,0:T(8,128)(2,1)S(1)} %copy-done, f32[64,2,128]{2,0,1:T(8,128)S(1)} %fusion.13), kind=kOutput, calls=%fused_computation.8 | convolution fusion | flops 25165824 | bytes 2228224 | tf_op jit(solution)/shard_map/tfb,tab->tfa/dot_general | solution.py:318
  86.8 0.0 copy-done.6
  86.8 0.2 convolution_bitcast_fusion
  87.0 0.7 copy.49
  87.7 1.1 %copy.51 = f32[80,2,16,128]{3,2,1,0:T(8,128)} copy(f32[80,2,16,128]{3,2,1,0:T(8,128)S(1)} %ocean.1) | data formatting | bytes 2621440
  (3 shorter events, 0.1 us)
Async XLA Ops:
  0.6 3.4 %copy-start = (bf16[64,128,128]{2,1,0:T(8,128)(2,1)S(1)}, bf16[64,128,128]{2,1,0:T(8,128)(2,1)}, u32[]{:S(2)}) copy-start(bf16[64,128,128]{2,1,0:T(8,128)(2,1)} %param.16) | copy-start | bytes 6291460
  4.0 19.3 %copy-start.1 = (f32[80,2,16,128]{3,2,1,0:T(8,128)S(1)}, f32[80,2,16,128]{3,2,1,0:T(8,128)}, u32[]{:S(2)}) copy-start(f32[80,2,16,128]{3,2,1,0:T(8,128)} %tracer.1) | copy-start | bytes 3932164
  4.0 19.3 %copy-start.4 = (s32[16,128]{1,0:T(8,128)S(1)}, s32[16,128]{1,0:T(8,128)}, u32[]{:S(2)}) copy-start(s32[16,128]{1,0:T(8,128)} %kmt.1) | copy-start | bytes 24580
  4.1 19.3 %copy-start.5 = (s32[16,128]{1,0:T(8,128)S(1)}, s32[16,128]{1,0:T(8,128)}, u32[]{:S(2)}) copy-start(s32[16,128]{1,0:T(8,128)} %land.1) | copy-start | bytes 24580
  23.4 1.3 %copy-start.2 = (f32[2,80,16,128]{3,2,1,0:T(8,128)S(1)}, f32[2,80,16,128]{3,2,1,0:T(8,128)}, u32[]{:S(2)}) copy-start(f32[2,80,16,128]{3,2,1,0:T(8,128)} %velocity.1) | copy-start | bytes 3932164
  24.7 1.1 %copy-start.3 = (f32[79,16,128]{2,1,0:T(8,128)S(1)}, f32[79,16,128]{2,1,0:T(8,128)}, u32[]{:S(2)}) copy-start(f32[79,16,128]{2,1,0:T(8,128)} %kappa.1) | copy-start | bytes 1941508
  71.6 15.2 %copy-start.6 = (s32[64]{0:T(128)S(1)}, s32[64]{0:T(128)}, u32[]{:S(2)}) copy-start(s32[64]{0:T(128)} %param.18) | copy-start | bytes 772
where the time goes:
time: 89 us; the launch traced here: 88.7 us
  Pallas kernels  45.9 us (52%)
  blocking collectives  27.6 us (31%)
  matrix products  7.29 us (8%)
  local copies, waits for them, and re-layouts  4.66 us (5%)
  other arithmetic  2.49 us (3%)
    pallas_call x1, Pallas kernels, ocean(): pl.pallas_call(functools.partial(ocean_kernel, n_blk, n_sub), out_shape=j...  45.9 us
    all_to_all x1, blocking collectives, local(): lax.all_to_all(outgoing.reshape(devices, capacity, ntracer + 1, cols), ('...  16.4 us
    all_to_all x1, blocking collectives, local(): lax.all_to_all(surface_rows.reshape(devices, capacity, ntracer, cols), ('...  11.2 us
    unnamed x16, local copies, waits for them, and re-layouts  4.14 us
    dot_general x1, matrix products, local(): back = jnp.einsum('tfb,tab->tfa', tile_values, weights32, precision=HIGH)  3.34 us

commit v1 on v0

--- a/solution.py
+++ b/solution.py
@@ -15,9 +15,9 @@
 
 
 def ocean_kernel(
-    n_blk, n_sub, tracer, velocity, kappa, kmt, land, flux, out,
-    cc, cw, ce, cn, cs, md, gg, inv, col_out, row_out, col_in, row_in,
-    col_send, row_send, col_recv, row_recv,
+    n_blk, n_sub, tracer, velocity, kappa, kmt, land, outgoing, out, returned,
+    cc, cw, ce, cn, cs, md, gg, inv, col_out, row_out, col_in, row_in, inbox, back_out, back_in,
+    col_send, row_send, col_recv, row_recv, flux_send, flux_recv, back_send, back_recv,
 ):
     levels, ntr, rows, cols = tracer.shape
     blk, sub = lax.axis_index("blk"), lax.axis_index("sub")
@@ -30,18 +30,41 @@
     zero = jnp.zeros((rows, cols), jnp.float32)
 
     barrier = pltpu.get_barrier_semaphore()
-    pl.semaphore_signal(barrier, inc=1, device_id=(east, sub), device_id_type=MESH)
-    pl.semaphore_signal(barrier, inc=1, device_id=(west, sub), device_id_type=MESH)
-
-    @pl.when(has_north)
-    def _():
-        pl.semaphore_signal(barrier, inc=1, device_id=(blk, north), device_id_type=MESH)
-
-    @pl.when(has_south)
-    def _():
-        pl.semaphore_signal(barrier, inc=1, device_id=(blk, south), device_id_type=MESH)
-
-    pl.semaphore_wait(barrier, 2 + has_north.astype(jnp.int32) + has_south.astype(jnp.int32))
+    devices, capacity = outgoing.shape[:2]
+    me = blk * n_sub + sub
+
+    def others(body):
+        def one(i, carry):
+            body(lax.rem(me + i, devices))
+            return carry
+
+        lax.fori_loop(1, devices, one, 0)
+
+    def place_of(device):
+        return (device // n_sub, lax.rem(device, n_sub))
+
+    others(lambda d: pl.semaphore_signal(barrier, inc=1, device_id=place_of(d), device_id_type=MESH))
+    pl.semaphore_wait(barrier, devices - 1)
+
+    def flux_copy(source, target):
+        return pltpu.make_async_remote_copy(
+            src_ref=outgoing.at[target],
+            dst_ref=inbox.at[source],
+            send_sem=flux_send.at[target],
+            recv_sem=flux_recv.at[source],
+            device_id=place_of(target),
+            device_id_type=MESH,
+        )
+
+    def back_copy(source, target):
+        return pltpu.make_async_remote_copy(
+            src_ref=back_out.at[target],
+            dst_ref=back_in.at[source],
+            send_sem=back_send.at[target],
+            recv_sem=back_recv.at[source],
+            device_id=place_of(target),
+            device_id_type=MESH,
+        )
 
     def col_copy(step, side, count):
         return pltpu.make_async_remote_copy(
@@ -140,6 +163,8 @@
         for side in range(2):
             col_out[0, side, f] = packed[2 * f + side]
     send(0, ntr + 1)
+    others(lambda d: flux_copy(me, d).start())
+    inbox[me] = outgoing[me]
 
     @pl.when(jnp.logical_not(has_north))
     def _():
@@ -191,6 +216,23 @@
     loop(stencil, 0)
     surface = jnp.where(land[...] > 0, FORCE, 0.0) * inv[0]
 
+    def add_flux(device, totals):
+        totals = list(totals)
+        for c in range(capacity):
+            message = inbox[device, pl.ds(c, 1), :]
+            here = row == message[:, ntr * cols:].astype(jnp.int32)
+            for f in range(ntr):
+                totals[f] += jnp.where(here, message[:, f * cols:(f + 1) * cols], 0.0)
+        return tuple(totals)
+
+    def answer(device, top):
+        for c in range(capacity):
+            here = row == inbox[device, pl.ds(c, 1), pl.ds(ntr * cols, cols)].astype(jnp.int32)
+            for f in range(ntr):
+                back_out[device, pl.ds(c, 1), pl.ds(f * cols, cols)] = jnp.sum(
+                    jnp.where(here, top[f], 0.0), axis=0, keepdims=True
+                )
+
     for step in range(NSTEP):
         if step:
             receive(step, ntr)
@@ -212,10 +254,22 @@
             return tuple(now)
 
         top = loop(forward, (zero,) * ntr, down=True)
+        if step == 0:
+            others(lambda d: flux_copy(d, me).wait_recv())
+            flux = lax.fori_loop(0, devices, add_flux, (zero,) * ntr)
+            flux = [surface * flux[f] for f in range(ntr)]
+        top = [top[f] + flux[f] for f in range(ntr)]
         for f in range(ntr):
-            out[0, f] = top[f] + surface * flux[f]
+            out[0, f] = top[f]
 
         last = step == NSTEP - 1
+        if last:
+            def reply(d):
+                answer(d, top)
+                back_copy(me, d).start()
+
+            others(reply)
+            answer(me, top)
 
         def backward(k, carry):
             carry = list(carry)
@@ -240,33 +294,47 @@
 
     for step in range(NSTEP):
         finish(step, ntr + 1 if step == 0 else ntr)
-
-
-def ocean(n_blk, n_sub, tracer, velocity, kappa, kmt, land, flux):
+    returned[me] = back_out[me]
+
+    def take(d):
+        back_copy(d, me).wait_recv()
+        returned[d] = back_in[d]
+
+    others(take)
+    others(lambda d: flux_copy(me, d).wait_send())
+    others(lambda d: back_copy(me, d).wait_send())
+
+
+def ocean(n_blk, n_sub, tracer, velocity, kappa, kmt, land, outgoing):
     levels, ntr, rows, cols = tracer.shape
+    devices, capacity = outgoing.shape[:2]
     field = pltpu.VMEM((levels, rows, cols), jnp.float32)
     vmem = pl.BlockSpec(memory_space=pltpu.VMEM)
     return pl.pallas_call(
         functools.partial(ocean_kernel, n_blk, n_sub),
-        out_shape=jax.ShapeDtypeStruct(tracer.shape, jnp.float32),
+        out_shape=(
+            jax.ShapeDtypeStruct(tracer.shape, jnp.float32),
+            jax.ShapeDtypeStruct((devices, capacity, ntr * cols), jnp.float32),
+        ),
         in_specs=[vmem] * 6,
-        out_specs=vmem,
+        out_specs=(vmem, vmem),
         scratch_shapes=[field] * 8
         + [
             pltpu.VMEM((NSTEP, 2, ntr + 1, rows, cols), jnp.float32),
             pltpu.VMEM((NSTEP, 2, ntr + 1, levels, cols), jnp.float32),
             pltpu.VMEM((NSTEP, 2, ntr + 1, rows, cols), jnp.float32),
             pltpu.VMEM((NSTEP, 2, ntr + 1, levels, cols), jnp.float32),
-            pltpu.SemaphoreType.DMA((NSTEP, 2)),
-            pltpu.SemaphoreType.DMA((NSTEP, 2)),
-            pltpu.SemaphoreType.DMA((NSTEP, 2)),
-            pltpu.SemaphoreType.DMA((NSTEP, 2)),
-        ],
+            pltpu.VMEM(outgoing.shape, jnp.float32),
+            pltpu.VMEM((devices, capacity, ntr * cols), jnp.float32),
+            pltpu.VMEM((devices, capacity, ntr * cols), jnp.float32),
+        ]
+        + [pltpu.SemaphoreType.DMA((NSTEP, 2))] * 4
+        + [pltpu.SemaphoreType.DMA((devices,))] * 4,
         compiler_params=pltpu.CompilerParams(
             collective_id=0, has_side_effects=True, vmem_limit_bytes=40 * 1024 * 1024
         ),
         name="ocean",
-    )(tracer, velocity, kappa, kmt, land, flux)
+    )(tracer, velocity, kappa, kmt, land, outgoing)
 
 
 def local(
@@ -294,25 +362,8 @@
     place = (slot_of[:, None] == jnp.arange(slots, dtype=jnp.int32)[None]).astype(jnp.float32)
     named = jnp.broadcast_to(remap_dst_block.astype(jnp.float32)[:, None, None], (tiles, 1, cols))
     outgoing = jnp.einsum("ts,tfc->sfc", place, jnp.concatenate([contrib, named], axis=1), precision=HIGH)
-    incoming = lax.all_to_all(
-        outgoing.reshape(devices, capacity, ntracer + 1, cols),
-        ("blk", "sub"),
-        split_axis=0,
-        concat_axis=0,
-        tiled=True,
-    ).reshape(slots, ntracer + 1, cols)
-    got_rows = incoming[:, ntracer, 0].astype(jnp.int32)
-    row_pick = (got_rows[:, None] == jnp.arange(rows, dtype=jnp.int32)[None]).astype(jnp.float32)
-    ocean_flux = jnp.einsum("sr,sfc->frc", row_pick, incoming[:, :ntracer], precision=HIGH)
-    ocean_state = ocean(n_blk, n_sub, tracer, velocity, kappa, kmt, land_mask, ocean_flux)
-    surface_rows = jnp.einsum("sr,frc->sfc", row_pick, ocean_state[0], precision=HIGH)
-    returned = lax.all_to_all(
-        surface_rows.reshape(devices, capacity, ntracer, cols),
-        ("blk", "sub"),
-        split_axis=0,
-        concat_axis=0,
-        tiled=True,
-    )
+    outgoing = outgoing.reshape(devices, capacity, (ntracer + 1) * cols)
+    ocean_state, returned = ocean(n_blk, n_sub, tracer, velocity, kappa, kmt, land_mask, outgoing)
     returned = returned.reshape(slots, ntracer, cols)
     tile_values = jnp.einsum("ts,sfc->tfc", place, returned, precision=HIGH)
     back = jnp.einsum("tfb,tab->tfa", tile_values, weights32, precision=HIGH)

time: 89 us -> 80.4 us (0.903)
  blocking collectives: 27.6 us -> 0 us
  Pallas kernels: 45.9 us -> 60.2 us
  local copies, waits for them, and re-layouts: 4.66 us -> 9.59 us
    all_to_all x2 -> x0, blocking collectives: 27.6 us -> none  [the longest x1 16.4 us: local(): lax.all_to_all(outgoing.reshape(devices, capacity, ntracer + 1, cols), ('...]
    pallas_call x1, Pallas kernels: 45.9 us -> 60.2 us  [ocean(): pl.pallas_call(functools.partial(ocean_kernel, n_blk, n_sub), out_shape=(...]
    reshape x1 -> x2, local copies, waits for them, and re-layouts: 0.04 us -> 2.5 us  [the longest x1 1.76 us: local(): outgoing = outgoing.reshape(devices, capacity, (ntracer + 1) * cols)]
    unnamed x16 -> x26, local copies, waits for them, and re-layouts: 4.14 us -> 6.12 us
    dot_general x1, matrix products: 0.23 us -> 1.14 us  [local(): tile_values = jnp.einsum('ts,sfc->tfc', place, returned, precision=HIGH)]
where the time goes in v1:
time: 80.4 us; the launch traced here: 80.1 us
  Pallas kernels  60.2 us (75%)
  local copies, waits for them, and re-layouts  9.59 us (12%)
  matrix products  7.79 us (10%)
  other arithmetic  1.78 us (2%)
    pallas_call x1, Pallas kernels, ocean(): pl.pallas_call(functools.partial(ocean_kernel, n_blk, n_sub), out_shape=(...  60.2 us
    unnamed x26, local copies, waits for them, and re-layouts  6.12 us
    dot_general x1, matrix products, local(): back = jnp.einsum('tfb,tab->tfa', tile_values, weights32, precision=HIGH)  3.33 us
    reshape x1, local copies, waits for them, and re-layouts, local(): outgoing = outgoing.reshape(devices, capacity, (ntracer + 1) * cols)  1.76 us
    dot_general x1, matrix products, local(): contrib = jnp.einsum('tfa,tab->tfb', blocks, weights32, precision=HIGH)  1.73 us

profile of v1, /device:TPU:0, one launch (start us, length us, event | category | flops | bytes accessed | tf_op | source)
XLA Modules:
  0.0 80.1 jit_solution(12312458098120748033)
XLA Ops:
  0.6 0.0 copy-start
  0.6 0.0 copy-start.11
  0.7 0.0 copy-start.1
  0.7 0.0 copy-start.7
  0.7 0.0 copy-start.8
  0.7 1.0 %convert_reduce_fusion = s32[64]{0:T(128)S(1)} fusion(s32[64]{0:T(128)} %bitcast.29), kind=kLoop, calls=%fused_computation.16 | loop fusion | flops 20416 | bytes 512 | tf_op jit(solution)/shard_map/reduce_sum | solution.py:360
  1.7 0.7 fusion.23
  2.4 0.0 copy-start.10
  2.4 1.0 %fusion.9 = f32[64,2,128]{2,0,1:T(8,128)S(1)} fusion(f32[1,2,48,128]{3,1,2,0:T(2,128)} %bitcast.27, s32[64]{0:T(128)} %param.18), kind=kOutput, calls=%fused_computation.12 | convolution fusion | flops 9440256 | bytes 114944 | tf_op jit(solution)/shard_map/tk,fkc->tfc/dot_general | solution.py:354
  3.5 0.0 copy-done
  3.5 1.7 %fusion.7 = f32[64,2,128]{2,1,0:T(2,128)S(1)} fusion(bf16[64,128,128]{2,1,0:T(8,128)(2,1)S(1)} %copy-done, f32[64,2,128]{2,0,1:T(8,128)S(1)} %fusion.9), kind=kOutput, calls=%fused_computation.9 | convolution fusion | flops 25165824 | bytes 2228224 | tf_op jit(solution)/shard_map/tfa,tab->tfb/dot_general | solution.py:355
  5.2 0.0 copy-done.11
  5.2 0.1 broadcast_in_dim.2
  5.3 0.1 pad_maximum_fusion
  5.4 0.4 fusion.2
  5.8 0.0 copy-done.10
  5.8 0.8 %copy.16 = f32[128,3,128]{2,1,0:T(4,128)} copy(f32[128,3,128]{2,0,1:T(8,128)S(1)} %fusion.2) | data formatting | bytes 393216 | tf_op jit(solution)/shard_map/ts,tfc->sfc/dot_general | solution.py:364
  6.6 1.8 %reshape.23.outgoing = f32[32,4,384]{2,1,0:T(4,128)} reshape(f32[128,3,128]{2,1,0:T(4,128)} %copy.16) | data formatting | bytes 393216 | tf_op jit(solution)/shard_map/reshape | solution.py:365
  8.4 0.0 copy-done.1
  8.4 0.0 copy-done.7
  8.4 0.0 copy-done.8
  8.4 0.0 copy-start.2
  8.4 1.3 %copy-done.2 = f32[2,80,16,128]{3,2,1,0:T(8,128)S(1)} copy-done((f32[2,80,16,128]{3,2,1,0:T(8,128)S(1)}, f32[2,80,16,128]{3,2,1,0:T(8,128)}, u32[]{:S(2)}) %copy-start.2) | copy-done | bytes 1310744
  9.7 0.0 copy-start.5
  9.7 0.9 %copy-done.5 = f32[32,4,384]{2,1,0:T(4,128)S(1)} copy-done((f32[32,4,384]{2,1,0:T(4,128)S(1)}, f32[32,4,384]{2,1,0:T(4,128)}, u32[]{:S(2)}) %copy-start.5) | copy-done | bytes 196632
  10.6 0.0 copy-start.6
  10.6 1.1 %copy-done.6 = f32[79,16,128]{2,1,0:T(8,128)S(1)} copy-done((f32[79,16,128]{2,1,0:T(8,128)S(1)}, f32[79,16,128]{2,1,0:T(8,128)}, u32[]{:S(2)}) %copy-start.6) | copy-done | bytes 647192
  11.7 60.2 %ocean.1 = (f32[80,2,16,128]{3,2,1,0:T(8,128)S(1)}, f32[32,4,256]{2,1,0:T(4,128)S(1)}) custom-call(f32[80,2,16,128]{3,2,1,0:T(8,128)S(1)} %copy-done.1, f32[2,80,16,128]{3,2,1,0:T(8,128)S(1)} %copy-done.2, f32[79,16,128]{2,1,0:T(8,128)S(1)} %copy-done.6, s32[16,128]{1,0:T(8,128)S(1)} %copy-done.7, s32[16,128]{1,0:T(8,128)S(1)} %copy-done.8, ...), custom_call_target="tpu_custom_call" | custom-call | tf_op jit(solution)/shard_map/ocean/pallas_call | solution.py:313
  71.9 0.0 copy-start.3
  71.9 1.0 %copy-done.3 = f32[80,2,16,128]{3,2,1,0:T(8,128)} copy-done((f32[80,2,16,128]{3,2,1,0:T(8,128)}, f32[80,2,16,128]{3,2,1,0:T(8,128)S(1)}, u32[]{:S(2)}) %copy-start.3) | copy-done | bytes 1310744
  73.0 0.0 copy-start.9
  73.0 0.0 copy-start.4
  73.0 0.7 reshape.24
  73.7 1.1 %fusion = f32[64,2,128]{2,0,1:T(8,128)S(1)} fusion(f32[128,2,128]{2,1,0:T(2,128)} %reshape.24, s32[64]{0:T(128)} %copy-done.10), kind=kOutput, calls=%fused_computation.2 | convolution fusion | flops 25174016 | bytes 196864 | tf_op jit(solution)/shard_map/ts,sfc->tfc/dot_general | solution.py:368
  74.9 3.3 %fusion.5 = f32[64,2,128]{2,1,0:T(2,128)S(1)} fusion(bf16[64,128,128]{2,1,0:T(8,128)(2,1)S(1)} %copy-done, f32[64,2,128]{2,0,1:T(8,128)S(1)} %fusion), kind=kOutput, calls=%fused_computation.7 | convolution fusion | flops 25165824 | bytes 2228224 | tf_op jit(solution)/shard_map/tfb,tab->tfa/dot_general | solution.py:369
  78.2 0.0 copy-done.9
  78.2 0.2 convolution_bitcast_fusion
  78.4 0.7 copy.37
  79.0 0.0 copy-done.4
  79.0 1.1 %copy.39 = f32[80,2,16,128]{3,2,1,0:T(8,128)} copy(f32[80,2,16,128]{3,2,1,0:T(8,128)S(1)} %copy-done.4) | data formatting | bytes 2621440
  (1 shorter events, 0.0 us)
Async XLA Ops:
  0.6 2.8 %copy-start = (bf16[64,128,128]{2,1,0:T(8,128)(2,1)S(1)}, bf16[64,128,128]{2,1,0:T(8,128)(2,1)}, u32[]{:S(2)}) copy-start(bf16[64,128,128]{2,1,0:T(8,128)(2,1)} %param.16) | copy-start | bytes 6291460
  0.6 4.5 %copy-start.11 = (s32[64]{0:T(128)S(1)}, s32[64]{0:T(128)}, u32[]{:S(2)}) copy-start(s32[64]{0:T(128)} %param.19) | copy-start | bytes 772
  0.7 7.7 %copy-start.1 = (f32[80,2,16,128]{3,2,1,0:T(8,128)S(1)}, f32[80,2,16,128]{3,2,1,0:T(8,128)}, u32[]{:S(2)}) copy-start(f32[80,2,16,128]{3,2,1,0:T(8,128)} %tracer.1) | copy-start | bytes 3932164
  0.7 7.7 %copy-start.7 = (s32[16,128]{1,0:T(8,128)S(1)}, s32[16,128]{1,0:T(8,128)}, u32[]{:S(2)}) copy-start(s32[16,128]{1,0:T(8,128)} %kmt.1) | copy-start | bytes 24580
  0.7 7.7 %copy-start.8 = (s32[16,128]{1,0:T(8,128)S(1)}, s32[16,128]{1,0:T(8,128)}, u32[]{:S(2)}) copy-start(s32[16,128]{1,0:T(8,128)} %land.1) | copy-start | bytes 24580
  2.4 3.4 %copy-start.10 = (s32[64]{0:T(128)}, s32[64]{0:T(128)S(1)}, u32[]{:S(2)}) copy-start(s32[64]{0:T(128)S(1)} %fusion.23) | copy-start | bytes 772
  8.4 1.3 %copy-start.2 = (f32[2,80,16,128]{3,2,1,0:T(8,128)S(1)}, f32[2,80,16,128]{3,2,1,0:T(8,128)}, u32[]{:S(2)}) copy-start(f32[2,80,16,128]{3,2,1,0:T(8,128)} %velocity.1) | copy-start | bytes 3932164
  9.7 0.9 %copy-start.5 = (f32[32,4,384]{2,1,0:T(4,128)S(1)}, f32[32,4,384]{2,1,0:T(4,128)}, u32[]{:S(2)}) copy-start(f32[32,4,384]{2,1,0:T(4,128)} %reshape.23.outgoing) | copy-start | bytes 589828
  10.6 1.1 %copy-start.6 = (f32[79,16,128]{2,1,0:T(8,128)S(1)}, f32[79,16,128]{2,1,0:T(8,128)}, u32[]{:S(2)}) copy-start(f32[79,16,128]{2,1,0:T(8,128)} %kappa.1) | copy-start | bytes 1941508
  71.9 1.1 %copy-start.3 = (f32[80,2,16,128]{3,2,1,0:T(8,128)}, f32[80,2,16,128]{3,2,1,0:T(8,128)S(1)}, u32[]{:S(2)}) copy-start(f32[80,2,16,128]{3,2,1,0:T(8,128)S(1)} %get-tuple-element.8) | copy-start | bytes 3932164
  73.0 5.2 %copy-start.9 = (s32[64]{0:T(128)S(1)}, s32[64]{0:T(128)}, u32[]{:S(2)}) copy-start(s32[64]{0:T(128)} %param.18) | copy-start | bytes 772
  73.0 6.1 %copy-start.4 = (f32[80,2,16,128]{3,2,1,0:T(8,128)S(1)}, f32[80,2,16,128]{3,2,1,0:T(8,128)}, u32[]{:S(2)}) copy-start(f32[80,2,16,128]{3,2,1,0:T(8,128)} %copy-done.3) | copy-start | bytes 3932164

commit v2 on v1

--- a/solution.py
+++ b/solution.py
@@ -11,7 +11,7 @@
 FORCE = 0.25
 HIGH = lax.Precision.HIGHEST
 MESH = pl.DeviceIdType.MESH
-UNROLL = 8
+UNROLL = 16
 
 
 def ocean_kernel(
@@ -240,20 +240,29 @@
         halo_e = [col_in[step, 0, f] for f in range(ntr)]
         halo_w = [col_in[step, 1, f] for f in range(ntr)]
 
-        def forward(k, carry):
-            now = []
-            for f in range(ntr):
-                value = state[k, f]
-                acc = cc[k] * value + md[k] * carry[f]
-                acc += cw[k] * west_of(value, halo_w[f], k)
-                acc += ce[k] * east_of(value, halo_e[f], k)
-                acc += cn[k] * north_of(value, row_in[step, 0, f, pl.ds(k, 1), :])
-                acc += cs[k] * south_of(value, row_in[step, 1, f, pl.ds(k, 1), :])
-                out[k, f] = acc
-                now.append(acc)
-            return tuple(now)
-
-        top = loop(forward, (zero,) * ntr, down=True)
+        def forward(i, carry):
+            ks = [levels - 1 - (i * unroll + j) for j in range(unroll)]
+            values = []
+            for k in ks:
+                for f in range(ntr):
+                    value = state[k, f]
+                    acc = cc[k] * value
+                    acc += cw[k] * west_of(value, halo_w[f], k)
+                    acc += ce[k] * east_of(value, halo_e[f], k)
+                    acc += cn[k] * north_of(value, row_in[step, 0, f, pl.ds(k, 1), :])
+                    acc += cs[k] * south_of(value, row_in[step, 1, f, pl.ds(k, 1), :])
+                    values.append(acc)
+            carry = list(carry)
+            for j, k in enumerate(ks):
+                for f in range(ntr):
+                    carry[f] = values[j * ntr + f] + md[k] * carry[f]
+                    values[j * ntr + f] = carry[f]
+            for j, k in enumerate(ks):
+                for f in range(ntr):
+                    out[k, f] = values[j * ntr + f]
+            return tuple(carry)
+
+        top = lax.fori_loop(0, levels // unroll, forward, (zero,) * ntr)
         if step == 0:
             others(lambda d: flux_copy(d, me).wait_recv())
             flux = lax.fori_loop(0, devices, add_flux, (zero,) * ntr)
@@ -271,21 +280,27 @@
             others(reply)
             answer(me, top)
 
-        def backward(k, carry):
+        def backward(i, carry):
+            ks = [i * unroll + j for j in range(unroll)]
             carry = list(carry)
-            for f in range(ntr):
-                value = out[k, f] + gg[k] * carry[f]
-                out[k, f] = value
-                carry[f] = value
-                if not last:
-                    for side in range(2):
-                        at = ntr + 2 * f + side
-                        carry[at] = put_col(carry[at], value, k, side)
-                    row_out[step + 1, 0, f, pl.ds(k, 1), :] = value[:1]
-                    row_out[step + 1, 1, f, pl.ds(k, 1), :] = value[rows - 1:]
+            values = [out[k, f] for k in ks for f in range(ntr)]
+            for j, k in enumerate(ks):
+                for f in range(ntr):
+                    carry[f] = values[j * ntr + f] + gg[k] * carry[f]
+                    values[j * ntr + f] = carry[f]
+            for j, k in enumerate(ks):
+                for f in range(ntr):
+                    value = values[j * ntr + f]
+                    out[k, f] = value
+                    if not last:
+                        for side in range(2):
+                            at = ntr + 2 * f + side
+                            carry[at] = put_col(carry[at], value, k, side)
+                        row_out[step + 1, 0, f, pl.ds(k, 1), :] = value[:1]
+                        row_out[step + 1, 1, f, pl.ds(k, 1), :] = value[rows - 1:]
             return tuple(carry)
 
-        done = loop(backward, (zero,) * (ntr if last else 3 * ntr))
+        done = lax.fori_loop(0, levels // unroll, backward, (zero,) * (ntr if last else 3 * ntr))
         if not last:
             for f in range(ntr):
                 for side in range(2):

time: 80.4 us -> 64.6 us (0.80)
  Pallas kernels: 60.2 us -> 44.3 us
    pallas_call x1, Pallas kernels: 60.2 us -> 44.3 us  [ocean(): pl.pallas_call(functools.partial(ocean_kernel, n_blk, n_sub), out_shape=(...]
where the time goes in v2:
time: 64.6 us; the launch traced here: 64.3 us
  Pallas kernels  44.3 us (69%)
  local copies, waits for them, and re-layouts  9.59 us (15%)
  matrix products  7.79 us (12%)
  other arithmetic  1.78 us (3%)
  between operations  0.77 us (1%)
    pallas_call x1, Pallas kernels, ocean(): pl.pallas_call(functools.partial(ocean_kernel, n_blk, n_sub), out_shape=(...  44.3 us
    unnamed x26, local copies, waits for them, and re-layouts  6.12 us
    dot_general x1, matrix products, local(): back = jnp.einsum('tfb,tab->tfa', tile_values, weights32, precision=HIGH)  3.33 us
    reshape x1, local copies, waits for them, and re-layouts, local(): outgoing = outgoing.reshape(devices, capacity, (ntracer + 1) * cols)  1.76 us
    dot_general x1, matrix products, local(): contrib = jnp.einsum('tfa,tab->tfb', blocks, weights32, precision=HIGH)  1.73 us

profile of v2, /device:TPU:0, one launch (start us, length us, event | category | flops | bytes accessed | tf_op | source)
XLA Modules:
  0.0 64.3 jit_solution(7777484817636297721)
XLA Ops:
  0.6 0.0 copy-start
  0.6 0.0 copy-start.11
  0.7 0.0 copy-start.1
  0.7 0.0 copy-start.7
  0.7 0.0 copy-start.8
  0.7 1.0 %convert_reduce_fusion = s32[64]{0:T(128)S(1)} fusion(s32[64]{0:T(128)} %bitcast.29), kind=kLoop, calls=%fused_computation.16 | loop fusion | flops 20416 | bytes 512 | tf_op jit(solution)/shard_map/reduce_sum | solution.py:375
  1.7 0.7 %fusion.23 = s32[64]{0:T(128)S(1)} fusion(s32[64]{0:T(128)S(1)} %convert_reduce_fusion, s32[64,1]{0,1:T(1,128)} %param.17), kind=kLoop, calls=%fused_computation.27 | loop fusion | flops 128 | bytes 768 | tf_op jit(solution)/shard_map/eq | solution.py:377
  2.4 0.0 copy-start.10
  2.4 1.0 %fusion.9 = f32[64,2,128]{2,0,1:T(8,128)S(1)} fusion(f32[1,2,48,128]{3,1,2,0:T(2,128)} %bitcast.27, s32[64]{0:T(128)} %param.18), kind=kOutput, calls=%fused_computation.12 | convolution fusion | flops 9440256 | bytes 114944 | tf_op jit(solution)/shard_map/tk,fkc->tfc/dot_general | solution.py:369
  3.5 0.0 copy-done
  3.5 1.7 %fusion.7 = f32[64,2,128]{2,1,0:T(2,128)S(1)} fusion(bf16[64,128,128]{2,1,0:T(8,128)(2,1)S(1)} %copy-done, f32[64,2,128]{2,0,1:T(8,128)S(1)} %fusion.9), kind=kOutput, calls=%fused_computation.9 | convolution fusion | flops 25165824 | bytes 2228224 | tf_op jit(solution)/shard_map/tfa,tab->tfb/dot_general | solution.py:370
  5.2 0.0 copy-done.11
  5.2 0.1 broadcast_in_dim.2
  5.3 0.1 pad_maximum_fusion
  5.4 0.4 fusion.2
  5.8 0.0 copy-done.10
  5.8 0.8 %copy.16 = f32[128,3,128]{2,1,0:T(4,128)} copy(f32[128,3,128]{2,0,1:T(8,128)S(1)} %fusion.2) | data formatting | bytes 393216 | tf_op jit(solution)/shard_map/ts,tfc->sfc/dot_general | solution.py:379
  6.6 1.8 %reshape.23.outgoing = f32[32,4,384]{2,1,0:T(4,128)} reshape(f32[128,3,128]{2,1,0:T(4,128)} %copy.16) | data formatting | bytes 393216 | tf_op jit(solution)/shard_map/reshape | solution.py:380
  8.4 0.0 copy-done.1
  8.4 0.0 copy-done.7
  8.4 0.0 copy-done.8
  8.4 0.0 copy-start.2
  8.4 1.3 %copy-done.2 = f32[2,80,16,128]{3,2,1,0:T(8,128)S(1)} copy-done((f32[2,80,16,128]{3,2,1,0:T(8,128)S(1)}, f32[2,80,16,128]{3,2,1,0:T(8,128)}, u32[]{:S(2)}) %copy-start.2) | copy-done | bytes 1310744
  9.7 0.0 copy-start.5
  9.7 0.9 %copy-done.5 = f32[32,4,384]{2,1,0:T(4,128)S(1)} copy-done((f32[32,4,384]{2,1,0:T(4,128)S(1)}, f32[32,4,384]{2,1,0:T(4,128)}, u32[]{:S(2)}) %copy-start.5) | copy-done | bytes 196632
  10.6 0.0 copy-start.6
  10.6 1.1 %copy-done.6 = f32[79,16,128]{2,1,0:T(8,128)S(1)} copy-done((f32[79,16,128]{2,1,0:T(8,128)S(1)}, f32[79,16,128]{2,1,0:T(8,128)}, u32[]{:S(2)}) %copy-start.6) | copy-done | bytes 647192
  11.7 44.3 %ocean.1 = (f32[80,2,16,128]{3,2,1,0:T(8,128)S(1)}, f32[32,4,256]{2,1,0:T(4,128)S(1)}) custom-call(f32[80,2,16,128]{3,2,1,0:T(8,128)S(1)} %copy-done.1, f32[2,80,16,128]{3,2,1,0:T(8,128)S(1)} %copy-done.2, f32[79,16,128]{2,1,0:T(8,128)S(1)} %copy-done.6, s32[16,128]{1,0:T(8,128)S(1)} %copy-done.7, s32[16,128]{1,0:T(8,128)S(1)} %copy-done.8, ...), custom_call_target="tpu_custom_call" | custom-call | tf_op jit(solution)/shard_map/ocean/pallas_call | solution.py:328
  56.1 0.0 copy-start.3
  56.1 1.0 %copy-done.3 = f32[80,2,16,128]{3,2,1,0:T(8,128)} copy-done((f32[80,2,16,128]{3,2,1,0:T(8,128)}, f32[80,2,16,128]{3,2,1,0:T(8,128)S(1)}, u32[]{:S(2)}) %copy-start.3) | copy-done | bytes 1310744
  57.1 0.0 copy-start.9
  57.1 0.0 copy-start.4
  57.1 0.7 %reshape.24 = f32[128,2,128]{2,1,0:T(2,128)} reshape(f32[32,4,256]{2,1,0:T(4,128)S(1)} %get-tuple-element.5) | data formatting | bytes 262144 | tf_op jit(solution)/shard_map/reshape | solution.py:382
  57.9 1.1 %fusion = f32[64,2,128]{2,0,1:T(8,128)S(1)} fusion(f32[128,2,128]{2,1,0:T(2,128)} %reshape.24, s32[64]{0:T(128)} %copy-done.10), kind=kOutput, calls=%fused_computation.2 | convolution fusion | flops 25174016 | bytes 196864 | tf_op jit(solution)/shard_map/ts,sfc->tfc/dot_general | solution.py:383
  59.0 3.3 %fusion.5 = f32[64,2,128]{2,1,0:T(2,128)S(1)} fusion(bf16[64,128,128]{2,1,0:T(8,128)(2,1)S(1)} %copy-done, f32[64,2,128]{2,0,1:T(8,128)S(1)} %fusion), kind=kOutput, calls=%fused_computation.7 | convolution fusion | flops 25165824 | bytes 2228224 | tf_op jit(solution)/shard_map/tfb,tab->tfa/dot_general | solution.py:384
  62.4 0.0 copy-done.9
  62.4 0.2 convolution_bitcast_fusion
  62.5 0.7 %copy.37 = f32[1,2,48,128]{3,1,2,0:T(2,128)} copy(f32[1,2,48,128]{3,2,1,0:T(8,128)S(1)} %convolution_bitcast_fusion) | data formatting | bytes 98304
  63.2 0.0 copy-done.4
  63.2 1.1 %copy.39 = f32[80,2,16,128]{3,2,1,0:T(8,128)} copy(f32[80,2,16,128]{3,2,1,0:T(8,128)S(1)} %copy-done.4) | data formatting | bytes 2621440
  (1 shorter events, 0.0 us)
Async XLA Ops:
  0.6 2.8 %copy-start = (bf16[64,128,128]{2,1,0:T(8,128)(2,1)S(1)}, bf16[64,128,128]{2,1,0:T(8,128)(2,1)}, u32[]{:S(2)}) copy-start(bf16[64,128,128]{2,1,0:T(8,128)(2,1)} %param.16) | copy-start | bytes 6291460
  0.6 4.5 %copy-start.11 = (s32[64]{0:T(128)S(1)}, s32[64]{0:T(128)}, u32[]{:S(2)}) copy-start(s32[64]{0:T(128)} %param.19) | copy-start | bytes 772
  0.7 7.7 %copy-start.1 = (f32[80,2,16,128]{3,2,1,0:T(8,128)S(1)}, f32[80,2,16,128]{3,2,1,0:T(8,128)}, u32[]{:S(2)}) copy-start(f32[80,2,16,128]{3,2,1,0:T(8,128)} %tracer.1) | copy-start | bytes 3932164
  0.7 7.7 %copy-start.7 = (s32[16,128]{1,0:T(8,128)S(1)}, s32[16,128]{1,0:T(8,128)}, u32[]{:S(2)}) copy-start(s32[16,128]{1,0:T(8,128)} %kmt.1) | copy-start | bytes 24580
  0.7 7.7 %copy-start.8 = (s32[16,128]{1,0:T(8,128)S(1)}, s32[16,128]{1,0:T(8,128)}, u32[]{:S(2)}) copy-start(s32[16,128]{1,0:T(8,128)} %land.1) | copy-start | bytes 24580
  2.4 3.4 %copy-start.10 = (s32[64]{0:T(128)}, s32[64]{0:T(128)S(1)}, u32[]{:S(2)}) copy-start(s32[64]{0:T(128)S(1)} %fusion.23) | copy-start | bytes 772
  8.4 1.3 %copy-start.2 = (f32[2,80,16,128]{3,2,1,0:T(8,128)S(1)}, f32[2,80,16,128]{3,2,1,0:T(8,128)}, u32[]{:S(2)}) copy-start(f32[2,80,16,128]{3,2,1,0:T(8,128)} %velocity.1) | copy-start | bytes 3932164
  9.7 0.9 %copy-start.5 = (f32[32,4,384]{2,1,0:T(4,128)S(1)}, f32[32,4,384]{2,1,0:T(4,128)}, u32[]{:S(2)}) copy-start(f32[32,4,384]{2,1,0:T(4,128)} %reshape.23.outgoing) | copy-start | bytes 589828
  10.6 1.1 %copy-start.6 = (f32[79,16,128]{2,1,0:T(8,128)S(1)}, f32[79,16,128]{2,1,0:T(8,128)}, u32[]{:S(2)}) copy-start(f32[79,16,128]{2,1,0:T(8,128)} %kappa.1) | copy-start | bytes 1941508
  56.1 1.1 %copy-start.3 = (f32[80,2,16,128]{3,2,1,0:T(8,128)}, f32[80,2,16,128]{3,2,1,0:T(8,128)S(1)}, u32[]{:S(2)}) copy-start(f32[80,2,16,128]{3,2,1,0:T(8,128)S(1)} %get-tuple-element.8) | copy-start | bytes 3932164
  57.1 5.2 %copy-start.9 = (s32[64]{0:T(128)S(1)}, s32[64]{0:T(128)}, u32[]{:S(2)}) copy-start(s32[64]{0:T(128)} %param.18) | copy-start | bytes 772
  57.1 6.1 %copy-start.4 = (f32[80,2,16,128]{3,2,1,0:T(8,128)S(1)}, f32[80,2,16,128]{3,2,1,0:T(8,128)}, u32[]{:S(2)}) copy-start(f32[80,2,16,128]{3,2,1,0:T(8,128)} %copy-done.3) | copy-start | bytes 3932164

commit v3 on v2

--- a/solution.py
+++ b/solution.py
@@ -50,8 +50,8 @@
         return pltpu.make_async_remote_copy(
             src_ref=outgoing.at[target],
             dst_ref=inbox.at[source],
-            send_sem=flux_send.at[target],
-            recv_sem=flux_recv.at[source],
+            send_sem=flux_send,
+            recv_sem=flux_recv,
             device_id=place_of(target),
             device_id_type=MESH,
         )
@@ -60,8 +60,8 @@
         return pltpu.make_async_remote_copy(
             src_ref=back_out.at[target],
             dst_ref=back_in.at[source],
-            send_sem=back_send.at[target],
-            recv_sem=back_recv.at[source],
+            send_sem=back_send,
+            recv_sem=back_recv,
             device_id=place_of(target),
             device_id_type=MESH,
         )
@@ -216,6 +216,27 @@
     loop(stencil, 0)
     surface = jnp.where(land[...] > 0, FORCE, 0.0) * inv[0]
 
+    def all_of(out_ref, in_ref, send_sem, recv_sem):
+        return pltpu.make_async_remote_copy(
+            src_ref=out_ref.at[pl.ds(0, devices - 1)],
+            dst_ref=in_ref.at[pl.ds(0, devices - 1)],
+            send_sem=send_sem,
+            recv_sem=recv_sem,
+            device_id=(east, sub),
+            device_id_type=MESH,
+        )
+
+    flux_all = all_of(outgoing, inbox, flux_send, flux_recv)
+    back_all = all_of(back_out, back_in, back_send, back_recv)
+
+    def grouped(body):
+        def group(i, carry):
+            for j in range(n_sub):
+                carry = body(i * n_sub + j, carry)
+            return carry
+
+        return group
+
     def add_flux(device, totals):
         totals = list(totals)
         for c in range(capacity):
@@ -232,6 +253,7 @@
                 back_out[device, pl.ds(c, 1), pl.ds(f * cols, cols)] = jnp.sum(
                     jnp.where(here, top[f], 0.0), axis=0, keepdims=True
                 )
+        return top
 
     for step in range(NSTEP):
         if step:
@@ -264,8 +286,8 @@
 
         top = lax.fori_loop(0, levels // unroll, forward, (zero,) * ntr)
         if step == 0:
-            others(lambda d: flux_copy(d, me).wait_recv())
-            flux = lax.fori_loop(0, devices, add_flux, (zero,) * ntr)
+            flux_all.wait_recv()
+            flux = lax.fori_loop(0, n_blk, grouped(add_flux), (zero,) * ntr)
             flux = [surface * flux[f] for f in range(ntr)]
         top = [top[f] + flux[f] for f in range(ntr)]
         for f in range(ntr):
@@ -273,12 +295,9 @@
 
         last = step == NSTEP - 1
         if last:
-            def reply(d):
-                answer(d, top)
-                back_copy(me, d).start()
-
-            others(reply)
-            answer(me, top)
+            lax.fori_loop(0, n_blk, grouped(answer), tuple(top))
+            others(lambda d: back_copy(me, d).start())
+            back_in[me] = back_out[me]
 
         def backward(i, carry):
             ks = [i * unroll + j for j in range(unroll)]
@@ -309,15 +328,10 @@
 
     for step in range(NSTEP):
         finish(step, ntr + 1 if step == 0 else ntr)
-    returned[me] = back_out[me]
-
-    def take(d):
-        back_copy(d, me).wait_recv()
-        returned[d] = back_in[d]
-
-    others(take)
-    others(lambda d: flux_copy(me, d).wait_send())
-    others(lambda d: back_copy(me, d).wait_send())
+    back_all.wait_recv()
+    returned[...] = back_in[...]
+    flux_all.wait_send()
+    back_all.wait_send()
 
 
 def ocean(n_blk, n_sub, tracer, velocity, kappa, kmt, land, outgoing):
@@ -344,7 +358,7 @@
             pltpu.VMEM((devices, capacity, ntr * cols), jnp.float32),
         ]
         + [pltpu.SemaphoreType.DMA((NSTEP, 2))] * 4
-        + [pltpu.SemaphoreType.DMA((devices,))] * 4,
+        + [pltpu.SemaphoreType.DMA] * 4,
         compiler_params=pltpu.CompilerParams(
             collective_id=0, has_side_effects=True, vmem_limit_bytes=40 * 1024 * 1024
         ),

time: 64.6 us -> 62.5 us (0.967)
  Pallas kernels: 44.3 us -> 42.3 us
    pallas_call x1, Pallas kernels: 44.3 us -> 42.3 us  [ocean(): pl.pallas_call(functools.partial(ocean_kernel, n_blk, n_sub), out_shape=(...]
where the time goes in v3:
time: 62.5 us; the launch traced here: 62.2 us
  Pallas kernels  42.3 us (68%)
  local copies, waits for them, and re-layouts  9.59 us (15%)
  matrix products  7.79 us (12%)
  other arithmetic  1.78 us (3%)
  between operations  0.77 us (1%)
    pallas_call x1, Pallas kernels, ocean(): pl.pallas_call(functools.partial(ocean_kernel, n_blk, n_sub), out_shape=(...  42.3 us
    unnamed x26, local copies, waits for them, and re-layouts  6.12 us
    dot_general x1, matrix products, local(): back = jnp.einsum('tfb,tab->tfa', tile_values, weights32, precision=HIGH)  3.33 us
    reshape x1, local copies, waits for them, and re-layouts, local(): outgoing = outgoing.reshape(devices, capacity, (ntracer + 1) * cols)  1.76 us
    dot_general x1, matrix products, local(): contrib = jnp.einsum('tfa,tab->tfb', blocks, weights32, precision=HIGH)  1.73 us

profile of v3, /device:TPU:0, one launch (start us, length us, event | category | flops | bytes accessed | tf_op | source)
XLA Modules:
  0.0 62.2 jit_solution(9963711650426624776)
XLA Ops:
  0.6 0.0 copy-start
  0.6 0.0 copy-start.11
  0.7 0.0 copy-start.1
  0.7 0.0 copy-start.7
  0.7 0.0 copy-start.8
  0.7 1.0 %convert_reduce_fusion = s32[64]{0:T(128)S(1)} fusion(s32[64]{0:T(128)} %bitcast.29), kind=kLoop, calls=%fused_computation.16 | loop fusion | flops 20416 | bytes 512 | tf_op jit(solution)/shard_map/reduce_sum | solution.py:389
  1.7 0.7 %fusion.23 = s32[64]{0:T(128)S(1)} fusion(s32[64]{0:T(128)S(1)} %convert_reduce_fusion, s32[64,1]{0,1:T(1,128)} %param.17), kind=kLoop, calls=%fused_computation.27 | loop fusion | flops 128 | bytes 768 | tf_op jit(solution)/shard_map/eq | solution.py:391
  2.4 0.0 copy-start.10
  2.4 1.0 %fusion.9 = f32[64,2,128]{2,0,1:T(8,128)S(1)} fusion(f32[1,2,48,128]{3,1,2,0:T(2,128)} %bitcast.27, s32[64]{0:T(128)} %param.18), kind=kOutput, calls=%fused_computation.12 | convolution fusion | flops 9440256 | bytes 114944 | tf_op jit(solution)/shard_map/tk,fkc->tfc/dot_general | solution.py:383
  3.5 0.0 copy-done
  3.5 1.7 %fusion.7 = f32[64,2,128]{2,1,0:T(2,128)S(1)} fusion(bf16[64,128,128]{2,1,0:T(8,128)(2,1)S(1)} %copy-done, f32[64,2,128]{2,0,1:T(8,128)S(1)} %fusion.9), kind=kOutput, calls=%fused_computation.9 | convolution fusion | flops 25165824 | bytes 2228224 | tf_op jit(solution)/shard_map/tfa,tab->tfb/dot_general | solution.py:384
  5.2 0.0 copy-done.11
  5.2 0.1 broadcast_in_dim.2
  5.3 0.1 pad_maximum_fusion
  5.4 0.4 fusion.2
  5.8 0.0 copy-done.10
  5.8 0.8 %copy.16 = f32[128,3,128]{2,1,0:T(4,128)} copy(f32[128,3,128]{2,0,1:T(8,128)S(1)} %fusion.2) | data formatting | bytes 393216 | tf_op jit(solution)/shard_map/ts,tfc->sfc/dot_general | solution.py:393
  6.6 1.8 %reshape.23.outgoing = f32[32,4,384]{2,1,0:T(4,128)} reshape(f32[128,3,128]{2,1,0:T(4,128)} %copy.16) | data formatting | bytes 393216 | tf_op jit(solution)/shard_map/reshape | solution.py:394
  8.4 0.0 copy-done.1
  8.4 0.0 copy-done.7
  8.4 0.0 copy-done.8
  8.4 0.0 copy-start.2
  8.4 1.3 %copy-done.2 = f32[2,80,16,128]{3,2,1,0:T(8,128)S(1)} copy-done((f32[2,80,16,128]{3,2,1,0:T(8,128)S(1)}, f32[2,80,16,128]{3,2,1,0:T(8,128)}, u32[]{:S(2)}) %copy-start.2) | copy-done | bytes 1310744
  9.7 0.0 copy-start.5
  9.7 0.9 %copy-done.5 = f32[32,4,384]{2,1,0:T(4,128)S(1)} copy-done((f32[32,4,384]{2,1,0:T(4,128)S(1)}, f32[32,4,384]{2,1,0:T(4,128)}, u32[]{:S(2)}) %copy-start.5) | copy-done | bytes 196632
  10.6 0.0 copy-start.6
  10.6 1.1 %copy-done.6 = f32[79,16,128]{2,1,0:T(8,128)S(1)} copy-done((f32[79,16,128]{2,1,0:T(8,128)S(1)}, f32[79,16,128]{2,1,0:T(8,128)}, u32[]{:S(2)}) %copy-start.6) | copy-done | bytes 647192
  11.7 42.3 %ocean.1 = (f32[80,2,16,128]{3,2,1,0:T(8,128)S(1)}, f32[32,4,256]{2,1,0:T(4,128)S(1)}) custom-call(f32[80,2,16,128]{3,2,1,0:T(8,128)S(1)} %copy-done.1, f32[2,80,16,128]{3,2,1,0:T(8,128)S(1)} %copy-done.2, f32[79,16,128]{2,1,0:T(8,128)S(1)} %copy-done.6, s32[16,128]{1,0:T(8,128)S(1)} %copy-done.7, s32[16,128]{1,0:T(8,128)S(1)} %copy-done.8, ...), custom_call_target="tpu_custom_call" | custom-call | tf_op jit(solution)/shard_map/ocean/pallas_call | solution.py:342
  54.0 0.0 copy-start.3
  54.0 1.0 %copy-done.3 = f32[80,2,16,128]{3,2,1,0:T(8,128)} copy-done((f32[80,2,16,128]{3,2,1,0:T(8,128)}, f32[80,2,16,128]{3,2,1,0:T(8,128)S(1)}, u32[]{:S(2)}) %copy-start.3) | copy-done | bytes 1310744
  55.1 0.0 copy-start.9
  55.1 0.0 copy-start.4
  55.1 0.7 %reshape.24 = f32[128,2,128]{2,1,0:T(2,128)} reshape(f32[32,4,256]{2,1,0:T(4,128)S(1)} %get-tuple-element.5) | data formatting | bytes 262144 | tf_op jit(solution)/shard_map/reshape | solution.py:396
  55.8 1.1 %fusion = f32[64,2,128]{2,0,1:T(8,128)S(1)} fusion(f32[128,2,128]{2,1,0:T(2,128)} %reshape.24, s32[64]{0:T(128)} %copy-done.10), kind=kOutput, calls=%fused_computation.2 | convolution fusion | flops 25174016 | bytes 196864 | tf_op jit(solution)/shard_map/ts,sfc->tfc/dot_general | solution.py:397
  57.0 3.3 %fusion.5 = f32[64,2,128]{2,1,0:T(2,128)S(1)} fusion(bf16[64,128,128]{2,1,0:T(8,128)(2,1)S(1)} %copy-done, f32[64,2,128]{2,0,1:T(8,128)S(1)} %fusion), kind=kOutput, calls=%fused_computation.7 | convolution fusion | flops 25165824 | bytes 2228224 | tf_op jit(solution)/shard_map/tfb,tab->tfa/dot_general | solution.py:398
  60.3 0.0 copy-done.9
  60.3 0.2 convolution_bitcast_fusion
  60.5 0.7 %copy.37 = f32[1,2,48,128]{3,1,2,0:T(2,128)} copy(f32[1,2,48,128]{3,2,1,0:T(8,128)S(1)} %convolution_bitcast_fusion) | data formatting | bytes 98304
  61.1 0.0 copy-done.4
  61.1 1.1 %copy.39 = f32[80,2,16,128]{3,2,1,0:T(8,128)} copy(f32[80,2,16,128]{3,2,1,0:T(8,128)S(1)} %copy-done.4) | data formatting | bytes 2621440
  (1 shorter events, 0.0 us)
Async XLA Ops:
  0.6 2.8 %copy-start = (bf16[64,128,128]{2,1,0:T(8,128)(2,1)S(1)}, bf16[64,128,128]{2,1,0:T(8,128)(2,1)}, u32[]{:S(2)}) copy-start(bf16[64,128,128]{2,1,0:T(8,128)(2,1)} %param.16) | copy-start | bytes 6291460
  0.6 4.5 %copy-start.11 = (s32[64]{0:T(128)S(1)}, s32[64]{0:T(128)}, u32[]{:S(2)}) copy-start(s32[64]{0:T(128)} %param.19) | copy-start | bytes 772
  0.7 7.7 %copy-start.1 = (f32[80,2,16,128]{3,2,1,0:T(8,128)S(1)}, f32[80,2,16,128]{3,2,1,0:T(8,128)}, u32[]{:S(2)}) copy-start(f32[80,2,16,128]{3,2,1,0:T(8,128)} %tracer.1) | copy-start | bytes 3932164
  0.7 7.7 %copy-start.7 = (s32[16,128]{1,0:T(8,128)S(1)}, s32[16,128]{1,0:T(8,128)}, u32[]{:S(2)}) copy-start(s32[16,128]{1,0:T(8,128)} %kmt.1) | copy-start | bytes 24580
  0.7 7.7 %copy-start.8 = (s32[16,128]{1,0:T(8,128)S(1)}, s32[16,128]{1,0:T(8,128)}, u32[]{:S(2)}) copy-start(s32[16,128]{1,0:T(8,128)} %land.1) | copy-start | bytes 24580
  2.4 3.4 %copy-start.10 = (s32[64]{0:T(128)}, s32[64]{0:T(128)S(1)}, u32[]{:S(2)}) copy-start(s32[64]{0:T(128)S(1)} %fusion.23) | copy-start | bytes 772
  8.4 1.3 %copy-start.2 = (f32[2,80,16,128]{3,2,1,0:T(8,128)S(1)}, f32[2,80,16,128]{3,2,1,0:T(8,128)}, u32[]{:S(2)}) copy-start(f32[2,80,16,128]{3,2,1,0:T(8,128)} %velocity.1) | copy-start | bytes 3932164
  9.7 0.9 %copy-start.5 = (f32[32,4,384]{2,1,0:T(4,128)S(1)}, f32[32,4,384]{2,1,0:T(4,128)}, u32[]{:S(2)}) copy-start(f32[32,4,384]{2,1,0:T(4,128)} %reshape.23.outgoing) | copy-start | bytes 589828
  10.6 1.1 %copy-start.6 = (f32[79,16,128]{2,1,0:T(8,128)S(1)}, f32[79,16,128]{2,1,0:T(8,128)}, u32[]{:S(2)}) copy-start(f32[79,16,128]{2,1,0:T(8,128)} %kappa.1) | copy-start | bytes 1941508
  54.0 1.1 %copy-start.3 = (f32[80,2,16,128]{3,2,1,0:T(8,128)}, f32[80,2,16,128]{3,2,1,0:T(8,128)S(1)}, u32[]{:S(2)}) copy-start(f32[80,2,16,128]{3,2,1,0:T(8,128)S(1)} %get-tuple-element.8) | copy-start | bytes 3932164
  55.1 5.2 %copy-start.9 = (s32[64]{0:T(128)S(1)}, s32[64]{0:T(128)}, u32[]{:S(2)}) copy-start(s32[64]{0:T(128)} %param.18) | copy-start | bytes 772
  55.1 6.1 %copy-start.4 = (f32[80,2,16,128]{3,2,1,0:T(8,128)S(1)}, f32[80,2,16,128]{3,2,1,0:T(8,128)}, u32[]{:S(2)}) copy-start(f32[80,2,16,128]{3,2,1,0:T(8,128)} %copy-done.3) | copy-start | bytes 3932164

commit v4 on v3

--- a/solution.py
+++ b/solution.py
@@ -9,7 +9,7 @@
 
 NSTEP = 4
 FORCE = 0.25
-HIGH = lax.Precision.HIGHEST
+HIGH = lax.Precision.HIGH
 MESH = pl.DeviceIdType.MESH
 UNROLL = 16
 

time: 62.5 us -> 60.8 us (0.973)
  matrix products: 7.79 us -> 6.08 us
    dot_general x1, matrix products: 3.33 us -> 2.26 us  [local(): back = jnp.einsum('tfb,tab->tfa', tile_values, weights32, precision=HIGH)]
where the time goes in v4:
time: 60.8 us; the launch traced here: 60.5 us
  Pallas kernels  42.3 us (70%)
  local copies, waits for them, and re-layouts  9.59 us (16%)
  matrix products  6.08 us (10%)
  other arithmetic  1.78 us (3%)
  between operations  0.76 us (1%)
    pallas_call x1, Pallas kernels, ocean(): pl.pallas_call(functools.partial(ocean_kernel, n_blk, n_sub), out_shape=(...  42.3 us
    unnamed x26, local copies, waits for them, and re-layouts  6.11 us
    dot_general x1, matrix products, local(): back = jnp.einsum('tfb,tab->tfa', tile_values, weights32, precision=HIGH)  2.26 us
    reshape x1, local copies, waits for them, and re-layouts, local(): outgoing = outgoing.reshape(devices, capacity, (ntracer + 1) * cols)  1.76 us

profile of v4, /device:TPU:0, one launch (start us, length us, event | category | flops | bytes accessed | tf_op | source)
XLA Modules:
  0.0 60.5 jit_solution(5205177319230153034)
XLA Ops:
  0.6 0.0 copy-start
  0.6 0.0 copy-start.11
  0.7 0.0 copy-start.1
  0.7 0.0 copy-start.7
  0.7 0.0 copy-start.8
  0.7 1.0 %convert_reduce_fusion = s32[64]{0:T(128)S(1)} fusion(s32[64]{0:T(128)} %bitcast.29), kind=kLoop, calls=%fused_computation.16 | loop fusion | flops 20416 | bytes 512 | tf_op jit(solution)/shard_map/reduce_sum | solution.py:389
  1.7 0.7 %fusion.23 = s32[64]{0:T(128)S(1)} fusion(s32[64]{0:T(128)S(1)} %convert_reduce_fusion, s32[64,1]{0,1:T(1,128)} %param.17), kind=kLoop, calls=%fused_computation.27 | loop fusion | flops 128 | bytes 768 | tf_op jit(solution)/shard_map/eq | solution.py:391
  2.4 0.0 copy-start.10
  2.4 1.0 %fusion.9 = f32[64,2,128]{2,0,1:T(8,128)S(1)} fusion(f32[1,2,48,128]{3,1,2,0:T(2,128)} %bitcast.27, s32[64]{0:T(128)} %param.18), kind=kOutput, calls=%fused_computation.12 | convolution fusion | flops 4721664 | bytes 114944 | tf_op jit(solution)/shard_map/tk,fkc->tfc/dot_general | solution.py:383
  3.4 0.0 copy-done
  3.4 1.2 %fusion.7 = f32[64,2,128]{2,1,0:T(2,128)S(1)} fusion(bf16[64,128,128]{2,1,0:T(8,128)(2,1)S(1)} %copy-done, f32[64,2,128]{2,0,1:T(8,128)S(1)} %fusion.9), kind=kOutput, calls=%fused_computation.9 | convolution fusion | flops 12582912 | bytes 2228224 | tf_op jit(solution)/shard_map/tfa,tab->tfb/dot_general | solution.py:384
  4.6 0.0 copy-done.11
  4.6 0.1 broadcast_in_dim.2
  4.8 0.1 pad_maximum_fusion
  4.8 0.3 fusion.2
  5.2 0.0 copy-done.10
  5.2 0.8 %copy.16 = f32[128,3,128]{2,1,0:T(4,128)} copy(f32[128,3,128]{2,0,1:T(8,128)S(1)} %fusion.2) | data formatting | bytes 393216 | tf_op jit(solution)/shard_map/ts,tfc->sfc/dot_general | solution.py:393
  6.0 1.8 %reshape.23.outgoing = f32[32,4,384]{2,1,0:T(4,128)} reshape(f32[128,3,128]{2,1,0:T(4,128)} %copy.16) | data formatting | bytes 393216 | tf_op jit(solution)/shard_map/reshape | solution.py:394
  7.8 0.0 copy-done.1
  7.8 0.0 copy-done.7
  7.8 0.0 copy-done.8
  7.8 0.0 copy-start.2
  7.8 1.3 %copy-done.2 = f32[2,80,16,128]{3,2,1,0:T(8,128)S(1)} copy-done((f32[2,80,16,128]{3,2,1,0:T(8,128)S(1)}, f32[2,80,16,128]{3,2,1,0:T(8,128)}, u32[]{:S(2)}) %copy-start.2) | copy-done | bytes 1310744
  9.1 0.0 copy-start.5
  9.1 0.9 %copy-done.5 = f32[32,4,384]{2,1,0:T(4,128)S(1)} copy-done((f32[32,4,384]{2,1,0:T(4,128)S(1)}, f32[32,4,384]{2,1,0:T(4,128)}, u32[]{:S(2)}) %copy-start.5) | copy-done | bytes 196632
  10.0 0.0 copy-start.6
  10.1 1.1 %copy-done.6 = f32[79,16,128]{2,1,0:T(8,128)S(1)} copy-done((f32[79,16,128]{2,1,0:T(8,128)S(1)}, f32[79,16,128]{2,1,0:T(8,128)}, u32[]{:S(2)}) %copy-start.6) | copy-done | bytes 647192
  11.1 42.3 %ocean.1 = (f32[80,2,16,128]{3,2,1,0:T(8,128)S(1)}, f32[32,4,256]{2,1,0:T(4,128)S(1)}) custom-call(f32[80,2,16,128]{3,2,1,0:T(8,128)S(1)} %copy-done.1, f32[2,80,16,128]{3,2,1,0:T(8,128)S(1)} %copy-done.2, f32[79,16,128]{2,1,0:T(8,128)S(1)} %copy-done.6, s32[16,128]{1,0:T(8,128)S(1)} %copy-done.7, s32[16,128]{1,0:T(8,128)S(1)} %copy-done.8, ...), custom_call_target="tpu_custom_call" | custom-call | tf_op jit(solution)/shard_map/ocean/pallas_call | solution.py:342
  53.4 0.0 copy-start.3
  53.4 1.0 %copy-done.3 = f32[80,2,16,128]{3,2,1,0:T(8,128)} copy-done((f32[80,2,16,128]{3,2,1,0:T(8,128)}, f32[80,2,16,128]{3,2,1,0:T(8,128)S(1)}, u32[]{:S(2)}) %copy-start.3) | copy-done | bytes 1310744
  54.5 0.0 copy-start.9
  54.5 0.0 copy-start.4
  54.5 0.7 %reshape.24 = f32[128,2,128]{2,1,0:T(2,128)} reshape(f32[32,4,256]{2,1,0:T(4,128)S(1)} %get-tuple-element.5) | data formatting | bytes 262144 | tf_op jit(solution)/shard_map/reshape | solution.py:396
  55.2 1.1 %fusion = f32[64,2,128]{2,0,1:T(8,128)S(1)} fusion(f32[128,2,128]{2,1,0:T(2,128)} %reshape.24, s32[64]{0:T(128)} %copy-done.10), kind=kOutput, calls=%fused_computation.2 | convolution fusion | flops 12591104 | bytes 196864 | tf_op jit(solution)/shard_map/ts,sfc->tfc/dot_general | solution.py:397
  56.4 2.3 %fusion.5 = f32[64,2,128]{2,1,0:T(2,128)S(1)} fusion(bf16[64,128,128]{2,1,0:T(8,128)(2,1)S(1)} %copy-done, f32[64,2,128]{2,0,1:T(8,128)S(1)} %fusion), kind=kOutput, calls=%fused_computation.7 | convolution fusion | flops 12582912 | bytes 2228224 | tf_op jit(solution)/shard_map/tfb,tab->tfa/dot_general | solution.py:398
  58.6 0.0 copy-done.9
  58.6 0.2 convolution_bitcast_fusion
  58.8 0.6 %copy.37 = f32[1,2,48,128]{3,1,2,0:T(2,128)} copy(f32[1,2,48,128]{3,2,1,0:T(8,128)S(1)} %convolution_bitcast_fusion) | data formatting | bytes 98304
  59.4 0.0 copy-done.4
  59.4 1.1 %copy.39 = f32[80,2,16,128]{3,2,1,0:T(8,128)} copy(f32[80,2,16,128]{3,2,1,0:T(8,128)S(1)} %copy-done.4) | data formatting | bytes 2621440
  (1 shorter events, 0.0 us)
Async XLA Ops:
  0.6 2.8 %copy-start = (bf16[64,128,128]{2,1,0:T(8,128)(2,1)S(1)}, bf16[64,128,128]{2,1,0:T(8,128)(2,1)}, u32[]{:S(2)}) copy-start(bf16[64,128,128]{2,1,0:T(8,128)(2,1)} %param.16) | copy-start | bytes 6291460
  0.6 4.0 %copy-start.11 = (s32[64]{0:T(128)S(1)}, s32[64]{0:T(128)}, u32[]{:S(2)}) copy-start(s32[64]{0:T(128)} %param.19) | copy-start | bytes 772
  0.7 7.1 %copy-start.1 = (f32[80,2,16,128]{3,2,1,0:T(8,128)S(1)}, f32[80,2,16,128]{3,2,1,0:T(8,128)}, u32[]{:S(2)}) copy-start(f32[80,2,16,128]{3,2,1,0:T(8,128)} %tracer.1) | copy-start | bytes 3932164
  0.7 7.1 %copy-start.7 = (s32[16,128]{1,0:T(8,128)S(1)}, s32[16,128]{1,0:T(8,128)}, u32[]{:S(2)}) copy-start(s32[16,128]{1,0:T(8,128)} %kmt.1) | copy-start | bytes 24580
  0.7 7.1 %copy-start.8 = (s32[16,128]{1,0:T(8,128)S(1)}, s32[16,128]{1,0:T(8,128)}, u32[]{:S(2)}) copy-start(s32[16,128]{1,0:T(8,128)} %land.1) | copy-start | bytes 24580
  2.4 2.8 %copy-start.10 = (s32[64]{0:T(128)}, s32[64]{0:T(128)S(1)}, u32[]{:S(2)}) copy-start(s32[64]{0:T(128)S(1)} %fusion.23) | copy-start | bytes 772
  7.8 1.3 %copy-start.2 = (f32[2,80,16,128]{3,2,1,0:T(8,128)S(1)}, f32[2,80,16,128]{3,2,1,0:T(8,128)}, u32[]{:S(2)}) copy-start(f32[2,80,16,128]{3,2,1,0:T(8,128)} %velocity.1) | copy-start | bytes 3932164
  9.1 0.9 %copy-start.5 = (f32[32,4,384]{2,1,0:T(4,128)S(1)}, f32[32,4,384]{2,1,0:T(4,128)}, u32[]{:S(2)}) copy-start(f32[32,4,384]{2,1,0:T(4,128)} %reshape.23.outgoing) | copy-start | bytes 589828
  10.0 1.1 %copy-start.6 = (f32[79,16,128]{2,1,0:T(8,128)S(1)}, f32[79,16,128]{2,1,0:T(8,128)}, u32[]{:S(2)}) copy-start(f32[79,16,128]{2,1,0:T(8,128)} %kappa.1) | copy-start | bytes 1941508
  53.4 1.1 %copy-start.3 = (f32[80,2,16,128]{3,2,1,0:T(8,128)}, f32[80,2,16,128]{3,2,1,0:T(8,128)S(1)}, u32[]{:S(2)}) copy-start(f32[80,2,16,128]{3,2,1,0:T(8,128)S(1)} %get-tuple-element.8) | copy-start | bytes 3932164
  54.5 4.1 %copy-start.9 = (s32[64]{0:T(128)S(1)}, s32[64]{0:T(128)}, u32[]{:S(2)}) copy-start(s32[64]{0:T(128)} %param.18) | copy-start | bytes 772
  54.5 4.9 %copy-start.4 = (f32[80,2,16,128]{3,2,1,0:T(8,128)S(1)}, f32[80,2,16,128]{3,2,1,0:T(8,128)}, u32[]{:S(2)}) copy-start(f32[80,2,16,128]{3,2,1,0:T(8,128)} %copy-done.3) | copy-start | bytes 3932164
